TPU v7x, 256 devices: a whole 4x4x8 slice. The times are simulated.
256 devices in a mesh: row: 8 (over z_lo, core), col: 32 (over y, z_hi, x).
Axes of the slice: x: 4, y: 4, z: 8 (z_hi: 2, z_lo: 4; z = z_hi * 4 + z_lo), core: 2. Of those that a mesh axis runs over, the one named last changes fastest.
Arguments:
- activations: bfloat16 [1024, 8192], P(('row', 'col')), may hold values from -6 to 6
- cotangent: bfloat16 [1024, 8192], P(('row', 'col')), may hold values from -1.5 to 1.5
- up_panels: bfloat16 [16, 128, 128, 128], P('row', 'col'), may hold values from -0.125 to 0.125
- down_panels: bfloat16 [16, 128, 128, 128], P('row', 'col'), may hold values from -0.09375 to 0.09375
- block_index: int32 [128, 16], P('col'), may hold values from 0 to 63, as said below
- block_count: int32 [128], P('col'), may hold values from 5 to 16, as said below
Outputs:
- outputs: bfloat16 [1024, 8192], P(('row', 'col'))
- grad_inputs: bfloat16 [1024, 8192], P(('row', 'col'))
- grad_up: bfloat16 [16, 128, 128, 128], P('row', 'col')
- grad_down: bfloat16 [16, 128, 128, 128], P('row', 'col')
Inputs may be any that keep to these rules, and one draw needn't show every extreme that they name: `block_index`: the 16 block numbers of one panel are distinct. `block_count`: some panel has all 16 slots live.
All inputs are finite; a program needn't handle non-finite values.
Results may differ from a plain program's by a relative error of at most 0.024.
Values may be sent and summed in bfloat16 or wider, within the bound.
No kernel may reach another device: no remote copies, remote signals or barrier semaphores. Data moves between devices by JAX's collectives and lax.ppermute only.
A program may use at most 128 MiB of HBM per device.

v0:
```python
import jax
import jax.numpy as jnp
from jax import lax
from jax.sharding import PartitionSpec as P

BLK = 128


def select_blocks(matrix, indices, panels, slot_count):
    row_count = matrix.shape[0]
    blocked = matrix.reshape(row_count, matrix.shape[1] // BLK, BLK)
    return jnp.take(blocked, indices, axis=1).reshape(row_count, panels, slot_count, BLK)


def shards(activations, cotangent, up_panels, down_panels, block_index, block_count):
    up_all, down_all = (
        lax.all_gather(up_panels, "row", axis=0, tiled=True),
        lax.all_gather(down_panels, "row", axis=0, tiled=True),
    )
    slot_count = up_all.shape[0]
    panels = up_all.shape[1]
    features = activations.shape[1]
    feature_blocks = features // BLK
    active = lax.broadcasted_iota(jnp.int32, (slot_count, panels), 0) < block_count[None, :]
    nothing = jnp.zeros((), jnp.bfloat16)
    up_blocks = jnp.where(active[:, :, None, None], up_all, nothing)
    down_blocks = jnp.where(active[:, :, None, None], down_all, nothing)
    indices = block_index.reshape(-1)
    selector = (indices[:, None] == lax.broadcasted_iota(jnp.int32, (1, feature_blocks), 1)).astype(
        jnp.bfloat16
    )
    selector = selector.reshape(panels, slot_count, feature_blocks)
    down_dense = jnp.einsum(
        "pkb,kpcu->pcbu", selector, down_blocks, preferred_element_type=jnp.float32
    )
    down_dense = down_dense.astype(jnp.bfloat16).reshape(panels * BLK, features)
    up_dense = jnp.einsum("pkb,kpdc->pcbd", selector, up_blocks, preferred_element_type=jnp.float32)
    up_dense = up_dense.astype(jnp.bfloat16).reshape(panels * BLK, features)
    gathered = lax.all_gather(activations, "col", axis=0, tiled=True)
    act_blocks = select_blocks(gathered, indices, panels, slot_count)
    preact = jnp.einsum("tpkd,kpdc->tpc", act_blocks, up_blocks, preferred_element_type=jnp.float32)
    gate_value = jax.nn.sigmoid(preact)
    hidden = (preact * gate_value).astype(jnp.bfloat16)
    derivative = gate_value * (1.0 + preact * (1.0 - gate_value))
    cot_whole = lax.all_gather(cotangent, "col", axis=0, tiled=True)
    cot_blocks = select_blocks(cot_whole, indices, panels, slot_count)
    grad_hidden = jnp.einsum(
        "tpku,kpcu->tpc", cot_blocks, down_blocks, preferred_element_type=jnp.float32
    )
    grad_pre = (grad_hidden * derivative).astype(jnp.bfloat16)
    row_total = hidden.shape[0]
    hidden_flat = hidden.reshape(row_total, panels * BLK)
    grad_flat = grad_pre.reshape(row_total, panels * BLK)
    chosen = hidden_flat
    outputs = lax.psum_scatter(
        jnp.dot(chosen, down_dense, preferred_element_type=jnp.float32).astype(jnp.bfloat16),
        "col",
        scatter_dimension=0,
        tiled=True,
    )
    chosen = grad_flat
    grad_inputs = lax.psum_scatter(
        jnp.dot(chosen, up_dense, preferred_element_type=jnp.float32).astype(jnp.bfloat16),
        "col",
        scatter_dimension=0,
        tiled=True,
    )
    up_grad = jnp.einsum("tpkd,tpc->kpdc", act_blocks, grad_pre, preferred_element_type=jnp.float32)
    down_grad = jnp.einsum("tpc,tpku->kpcu", hidden, cot_blocks, preferred_element_type=jnp.float32)
    zero_float = jnp.zeros((), jnp.float32)
    up_grad = jnp.where(active[:, :, None, None], up_grad, zero_float)
    down_grad = jnp.where(active[:, :, None, None], down_grad, zero_float)
    shares = lax.psum_scatter(
        jnp.stack([up_grad, down_grad], axis=1).astype(jnp.bfloat16),
        "row",
        scatter_dimension=0,
        tiled=True,
    ).astype(jnp.float32)
    return (
        outputs,
        grad_inputs,
        shares[:, 0].astype(jnp.bfloat16),
        shares[:, 1].astype(jnp.bfloat16),
    )


def solution(mesh):
    in_specs = (
        P(("row", "col"), None),
        P(("row", "col"), None),
        P("row", "col", None, None),
        P("row", "col", None, None),
        P("col", None),
        P("col"),
    )
    out_specs = (
        P(("row", "col"), None),
        P(("row", "col"), None),
        P("row", "col", None, None),
        P("row", "col", None, None),
    )
    return jax.shard_map(shards, mesh=mesh, in_specs=in_specs, out_specs=out_specs, check_vma=False)
```

profile of v0, /device:TPU:2, one launch (start us, length us, event | category | flops | bytes accessed | tf_op | source)
XLA Modules:
  0.0 862.3 jit_solution(1691659319800014761)
XLA Ops:
  7.2 1.8 copy.43
  9.1 1.8 copy.45
  12.3 0.8 reshape.68
  13.8 38.6 %all-gather.7.cloned.1.call-done = bf16[16,4,128,128]{2,3,0,1:T(8,128)(2,1)} async-done(((bf16[2,4,128,128]{2,3,0,1:T(8,128)(2,1)}), bf16[16,4,128,128]{2,3,0,1:T(8,128)(2,1)}) %all-gather.7.cloned.1.call-update) | async-done | bytes 2097168 | tf_op jit(solution)/shard_map/all_gather | solution.py:17
  52.4 41.0 %all-gather.9.cloned.1.call-done = bf16[16,4,128,128]{2,3,0,1:T(8,128)(2,1)} async-done(((bf16[2,4,128,128]{2,3,0,1:T(8,128)(2,1)}), bf16[16,4,128,128]{2,3,0,1:T(8,128)(2,1)}) %all-gather.9.cloned.1.call-update) | async-done | bytes 2097168 | tf_op jit(solution)/shard_map/all_gather | solution.py:18
  93.4 4.5 broadcast_select_fusion.2
  97.9 89.3 %all-gather.11.cloned.1.call-done = bf16[32,4,8192]{2,1,0:T(4,128)(2,1)} async-done(((bf16[1,4,8192]{2,1,0:T(4,128)(2,1)}), bf16[32,4,8192]{2,1,0:T(4,128)(2,1)}) %all-gather.11.cloned.1.call-update) | async-done | bytes 2097168 | tf_op jit(solution)/shard_map/all_gather | solution.py:39
  187.2 4.9 reshape.67
  192.1 2.9 copy.44
  195.1 81.2 %all-gather.13.cloned.1.call-done = bf16[32,4,8192]{2,1,0:T(4,128)(2,1)} async-done(((bf16[1,4,8192]{2,1,0:T(4,128)(2,1)}), bf16[32,4,8192]{2,1,0:T(4,128)(2,1)}) %all-gather.13.cloned.1.call-update) | async-done | bytes 2097168 | tf_op jit(solution)/shard_map/all_gather | solution.py:45
  276.3 4.9 reshape.72
  281.1 4.3 copy.47
  285.4 3.8 gather_fusion.1
  289.2 2.2 gather_fusion
  291.4 2.8 broadcast_select_fusion
  295.0 1.1 fusion.7
  296.5 0.9 fusion.9
  298.2 2.4 pad_maximum_fusion
  300.8 3.4 copy.46
  304.2 4.7 copy.49
  308.9 7.3 convert_bitcast_fusion
  316.2 13.6 %copy.50 = bf16[4,128,64,128]{3,2,1,0:T(8,128)(2,1)} copy(bf16[4,128,64,128]{1,2,3,0:T(8,128)(2,1)} %convert_bitcast_fusion) | data formatting | bytes 16777216 | tf_op jit(solution)/shard_map/convert_element_type | solution.py:38
  329.7 2.4 convolution_convert_fusion.2
  332.2 1.0 copy-done
  333.2 6.7 convolution_convert_fusion
  339.9 6.7 convolution_convert_fusion.1
  349.8 55.4 %all-reduce.7.cloned.1.call-done = bf16[16,2,4,128,128]{3,4,0,2,1:T(8,128)(2,1)} async-done(((bf16[16,2,4,128,128]{3,4,0,2,1:T(8,128)(2,1)}), bf16[16,2,4,128,128]{3,4,0,2,1:T(8,128)(2,1)}) %all-reduce.7.cloned.1.call-update) | async-done | bytes 4194320
  405.2 1.1 dynamic-slice_bitcast_fusion
  406.3 0.9 copy.54
  407.1 0.8 copy.53
  408.0 445.8 %all-reduce.9.cloned.1.call-done = (bf16[128,8192]{1,0:T(8,128)(2,1)}, bf16[128,8192]{1,0:T(8,128)(2,1)}) async-done(((bf16[128,8192]{1,0:T(8,128)(2,1)}, bf16[128,8192]{1,0:T(8,128)(2,1)}), (bf16[128,8192]{1,0:T(8,128)(2,1)}, bf16[128,8192]{1,0:T(8,128)(2,1)})) %all-reduce.9.cloned.1.call-update) | async-done | bytes 4194320
  853.8 1.7 constant_dynamic-slice_fusion
  (31 shorter events, 6.2 us)
Async XLA Ops:
  7.2 45.2 %all-gather.7.cloned.1.call-start = ((), (), s32[]{:S(2)}) async-start(), calls=%async_computation | async-start | bytes 2359296 | tf_op jit(solution)/shard_map/all_gather | solution.py:17
  9.0 84.4 %all-gather.9.cloned.1.call-start = ((), (), s32[]{:S(2)}) async-start(), calls=%async_computation.1 | async-start | bytes 2359296 | tf_op jit(solution)/shard_map/all_gather | solution.py:18
  10.9 176.3 %all-gather.11.cloned.1.call-start = ((), (), s32[]{:S(2)}) async-start(), calls=%async_computation.2 | async-start | bytes 2162688 | tf_op jit(solution)/shard_map/all_gather | solution.py:39
  11.6 264.6 %all-gather.13.cloned.1.call-start = ((), (), s32[]{:S(2)}) async-start(), calls=%async_computation.3 | async-start | bytes 2162688 | tf_op jit(solution)/shard_map/all_gather | solution.py:45
  12.2 393.0 %all-reduce.7.cloned.1.call-start = ((), (), s32[]{:S(2)}) async-start(), calls=%async_computation.4 | async-start | bytes 8388608
  291.4 2.9 copy-start.1
  295.0 1.6 copy-start.2
  300.6 553.2 %all-reduce.9.cloned.1.call-start = ((), (), s32[]{:S(2)}) async-start(), calls=%async_computation.5 | async-start | bytes 8388608
  304.2 4.7 copy-start.3
  329.7 3.5 copy-start
  346.6 0.7 copy-start.5
  346.6 1.3 copy-start.4
Sparse Core Ops, SparseCore 0:
  10.4 41.9 all-gather.6
  54.7 38.6 all-gather.8
  96.9 90.2 all-gather.10
  190.6 85.6 all-gather.12
  300.7 104.4 all-reduce.6
  407.7 445.9 all-reduce.8
where the time goes:
time: 864 us; the launch traced here: 862 us
  waiting for transfers between devices  753 us (87%)
  local copies, waits for them, and re-layouts  56.7 us (7%)
  matrix products  26.6 us (3%)
  between operations  15.5 us (2%)
  other arithmetic  10.5 us (1%)
    unnamed x8, waiting for transfers between devices  502 us
    all_gather x1, waiting for transfers between devices, shards(): gathered = lax.all_gather(activations, 'col', axis=0, tiled=True)  89.3 us
    all_gather x1, waiting for transfers between devices, shards(): cot_whole = lax.all_gather(cotangent, 'col', axis=0, tiled=True)  81.2 us
    all_gather x1, waiting for transfers between devices, shards(): lax.all_gather(down_panels, 'row', axis=0, tiled=True)  41 us
    all_gather x1, waiting for transfers between devices, shards(): lax.all_gather(up_panels, 'row', axis=0, tiled=True)  38.6 us
  transfers between devices with their start and end apart: 6, of which 6 were waited for; matrix products, arithmetic and copies ran while one was open for 7% of the time, Pallas kernels for 0%

commit v1 on v0

v1 whole, which is shorter than its diff:
```python
import functools

import jax
import jax.numpy as jnp
from jax import lax
from jax.experimental import pallas as pl
from jax.experimental.pallas import tpu as pltpu
from jax.sharding import PartitionSpec as P

BLK = 128
NX, NY, NZ = 4, 4, 2
BF = jnp.bfloat16
F32 = jnp.float32
NT = (((1,), (1,)), ((), ()))
TN = (((0,), (0,)), ((), ()))


def col_index(y, z, x):
    return ((y % NY) * NZ + z % NZ) * NX + x % NX


def send(value, dy, dz, dx):
    pairs = [
        (col_index(y, z, x), col_index(y + dy, z + dz, x + dx))
        for y in range(NY)
        for z in range(NZ)
        for x in range(NX)
    ]
    return lax.ppermute(value, "col", pairs)


def fetch(value, dy, dz, dx):
    return send(value, -dy, -dz, -dx)


def block_kernel(slots, panels, *refs):
    index, count = refs[:2]
    act_in, cot_in, weights_in = refs[2:6], refs[6:10], refs[10]
    out_refs, gin_refs, grads = refs[11:15], refs[15:19], refs[19]
    act, cot, weights, out_sum, in_sum, a_cat, c_cat, up_cat, down_cat, sems = refs[20:]
    copies = []
    for d in range(4):
        copies.append(pltpu.make_async_copy(act_in[d], act.at[d], sems.at[d]))
        copies.append(pltpu.make_async_copy(cot_in[d], cot.at[:, d], sems.at[4 + d]))
    copies.append(pltpu.make_async_copy(weights_in, weights, sems.at[8]))
    for copy in copies:
        copy.start()
    out_sum[...] = jnp.zeros_like(out_sum)
    in_sum[...] = jnp.zeros_like(in_sum)
    for copy in copies:
        copy.wait()
    rows = act.shape[0] * act.shape[1] * act.shape[2]

    def one_panel(p, carry):
        live = count[p]
        for k in range(slots):
            r, s = k // 2, k % 2
            lanes = pl.ds(pl.multiple_of(index[p, k] * BLK, BLK), BLK)
            here = slice(k * BLK, (k + 1) * BLK)
            a_cat[:, here] = act[:, :, :, lanes].reshape(rows, BLK)
            c_cat[:, here] = cot[:, :, :, lanes].reshape(rows, BLK)
            up = weights[r, 0, s, p]
            down = weights[r, 1, s, p]
            up_cat[here, :] = jnp.where(k < live, up, jnp.zeros_like(up))
            down_cat[:, here] = jnp.where(k < live, down, jnp.zeros_like(down))
        preact = jnp.dot(a_cat[...], up_cat[...], preferred_element_type=F32)
        gate = jax.nn.sigmoid(preact)
        hidden = (preact * gate).astype(BF)
        derivative = gate * (1.0 + preact * (1.0 - gate))
        grad_hidden = lax.dot_general(c_cat[...], down_cat[...], NT, preferred_element_type=F32)
        grad_pre = (grad_hidden * derivative).astype(BF)
        spread = jnp.dot(hidden, down_cat[...], preferred_element_type=F32)
        spread_in = lax.dot_general(grad_pre, up_cat[...], NT, preferred_element_type=F32)
        up_grad = lax.dot_general(a_cat[...], grad_pre, TN, preferred_element_type=F32)
        down_grad = lax.dot_general(hidden, c_cat[...], TN, preferred_element_type=F32)
        for k in range(slots):
            r, s = k // 2, k % 2
            lanes = pl.ds(pl.multiple_of(index[p, k] * BLK, BLK), BLK)
            here = slice(k * BLK, (k + 1) * BLK)
            out_sum[:, lanes] += spread[:, here]
            in_sum[:, lanes] += spread_in[:, here]
            up_here, down_here = up_grad[here, :], down_grad[:, here]
            grads[r, 0, s, p] = jnp.where(k < live, up_here, 0.0).astype(BF)
            grads[r, 1, s, p] = jnp.where(k < live, down_here, 0.0).astype(BF)
        return carry

    lax.fori_loop(0, panels, one_panel, 0)
    for d in range(4):
        for e in range(4):
            place = pl.ds((d * 4 + e) * 8, 8)
            out_refs[d][e] = out_sum[place, :].astype(BF)
            gin_refs[e][d] = in_sum[place, :].astype(BF)


def block_products(index, count, act_parts, cot_parts, weights):
    panels, slots = index.shape
    part = act_parts[0].shape
    features = part[-1]
    rows = 4 * part[0] * part[1]
    any_space = pl.BlockSpec(memory_space=pl.ANY)
    smem = pl.BlockSpec(memory_space=pltpu.SMEM)
    vmem = pl.BlockSpec(memory_space=pltpu.VMEM)
    return pl.pallas_call(
        functools.partial(block_kernel, slots, panels),
        out_shape=[jax.ShapeDtypeStruct(part, BF)] * 8 + [jax.ShapeDtypeStruct(weights.shape, BF)],
        in_specs=[smem, smem] + [any_space] * 9,
        out_specs=[vmem] * 9,
        scratch_shapes=[
            pltpu.VMEM((4,) + part, BF),
            pltpu.VMEM((4,) + part, BF),
            pltpu.VMEM(weights.shape, BF),
            pltpu.VMEM((rows, features), F32),
            pltpu.VMEM((rows, features), F32),
            pltpu.VMEM((rows, slots * BLK), BF),
            pltpu.VMEM((rows, slots * BLK), BF),
            pltpu.VMEM((slots * BLK, BLK), BF),
            pltpu.VMEM((BLK, slots * BLK), BF),
            pltpu.SemaphoreType.DMA((9,)),
        ],
        compiler_params=pltpu.CompilerParams(vmem_limit_bytes=52 * 2**20),
        cost_estimate=pl.CostEstimate(flops=1_700_000_000, bytes_accessed=17_000_000, transcendentals=65536),
    )(index, count, *act_parts, *cot_parts, weights)


def total(terms):
    result = terms[0].astype(F32)
    for term in terms[1:]:
        result = result + term.astype(F32)
    return result


def shards(activations, cotangent, up_panels, down_panels, block_index, block_count):
    own_slots, panels = up_panels.shape[:2]
    own_weights = jnp.concatenate([up_panels.reshape(-1, BLK), down_panels.reshape(-1, BLK)])
    weights = lax.all_gather(own_weights, "row", axis=0, tiled=True)
    weights = weights.reshape(-1, 2, own_slots, panels, BLK, BLK)

    far = fetch(jnp.stack([activations, cotangent]), 0, 1, 0)
    act = jnp.concatenate([activations, far[0]])
    cot = jnp.concatenate([cotangent, far[1]])
    act = jnp.stack([act] + [fetch(act, 0, 0, d) for d in (1, 2, 3)])
    cot = jnp.stack([cot] + [fetch(cot, d, 0, 0) for d in (1, 2, 3)])
    act_parts = [act] + [fetch(act, d, 0, 0) for d in (1, 2, 3)]
    cot_parts = [cot] + [fetch(cot, 0, 0, d) for d in (1, 2, 3)]

    results = block_products(block_index, block_count, act_parts, cot_parts, weights)
    out_parts, in_parts, grads = results[:4], results[4:8], results[8]

    shares = lax.psum_scatter(grads.reshape(-1, BLK), "row", scatter_dimension=0, tiled=True)
    shares = shares.reshape(2, own_slots, panels, BLK, BLK)

    out = total([out_parts[0]] + [send(out_parts[d], d, 0, 0) for d in (1, 2, 3)]).astype(BF)
    gin = total([in_parts[0]] + [send(in_parts[d], 0, 0, d) for d in (1, 2, 3)]).astype(BF)
    out = total([out[0]] + [send(out[d], 0, 0, d) for d in (1, 2, 3)]).astype(BF)
    gin = total([gin[0]] + [send(gin[d], d, 0, 0) for d in (1, 2, 3)]).astype(BF)
    far = send(jnp.stack([out[4:], gin[4:]]), 0, 1, 0)
    outputs = total([out[:4], far[0]]).astype(BF)
    grad_inputs = total([gin[:4], far[1]]).astype(BF)
    return outputs, grad_inputs, shares[0], shares[1]


def solution(mesh):
    tokens = P(("row", "col"), None)
    blocks = P("row", "col", None, None)
    in_specs = (tokens, tokens, blocks, blocks, P("col", None), P("col"))
    out_specs = (tokens, tokens, blocks, blocks)
    return jax.shard_map(shards, mesh=mesh, in_specs=in_specs, out_specs=out_specs, check_vma=False)
```

time: 864 us -> 160 us (0.19)
  waiting for transfers between devices: 753 us -> 63.2 us
  starting transfers between devices: 0.42 us -> 57.7 us
  local copies, waits for them, and re-layouts: 56.7 us -> 3.7 us
  matrix products: 26.6 us -> 0 us
  Pallas kernels: 0 us -> 12.9 us
    unnamed x8 -> x2, waiting for transfers between devices: 502 us -> 0.03 us
    all_gather x4 -> x1, waiting for transfers between devices: 250 us -> 0.03 us  [shards(): weights = lax.all_gather(own_weights, 'row', axis=0, tiled=True)]
    ppermute x0 -> x26, starting transfers between devices: none -> 57.7 us  [send(): return lax.ppermute(value, 'col', pairs)]
    ppermute x0 -> x26, waiting for transfers between devices: none -> 49.5 us  [send(): return lax.ppermute(value, 'col', pairs)]
    dot_general x8 -> x0, matrix products: 26.6 us -> none  [the longest x1 7.29 us: shards(): jnp.einsum('pkb,kpdc->pcbd', selector, up_blocks, preferred_element_type=...]
    reshape x5 -> x0, local copies, waits for them, and re-layouts: 17.7 us -> none  [the longest x4 17 us: select_blocks(): blocked = matrix.reshape(row_count, matrix.shape[1] // BLK, BLK)]
    convert_element_type x2 -> x0, local copies, waits for them, and re-layouts: 14.6 us -> none  [the longest x1 13.6 us: shards(): up_dense = up_dense.astype(jnp.bfloat16).reshape(panels * BLK, features)]
    reduce_scatter x0 -> x1, waiting for transfers between devices: none -> 13.7 us  [shards(): lax.psum_scatter(grads.reshape(-1, BLK), 'row', scatter_dimension=0, tile...]
  transfers between devices with their start and end apart: 6 -> 28, of which waited for: 6 -> 13; matrix products, arithmetic and copies ran while one was open for 7% -> 4% of each run, Pallas kernels for 0% -> 0%
where the time goes in v1:
time: 160 us; the launch traced here: 159 us
  waiting for transfers between devices  63.2 us (40%)
  starting transfers between devices  57.7 us (36%)
  between operations  14.3 us (9%)
  Pallas kernels  12.9 us (8%)
  other arithmetic  7.31 us (5%)
  local copies, waits for them, and re-layouts  3.7 us (2%)
    ppermute x26, starting transfers between devices, send(): return lax.ppermute(value, 'col', pairs)  57.7 us
    ppermute x26, waiting for transfers between devices, send(): return lax.ppermute(value, 'col', pairs)  49.5 us
    reduce_scatter x1, waiting for transfers between devices, shards(): lax.psum_scatter(grads.reshape(-1, BLK), 'row', scatter_dimension=0, tile...  13.7 us
    pallas_call x1, Pallas kernels, block_products(): pl.pallas_call(functools.partial(block_kernel, slots, panels), out_shape=...  12.9 us
  transfers between devices with their start and end apart: 28, of which 13 were waited for; matrix products, arithmetic and copies ran while one was open for 4% of the time, Pallas kernels for 0%

profile of v1, /device:TPU:2, one launch (start us, length us, event | category | flops | bytes accessed | tf_op | source)
XLA Modules:
  0.0 159.2 jit_solution(18331963493699320853)
XLA Ops:
  7.2 1.9 %pad_maximum_fusion.2 = bf16[2048,128]{1,0:T(8,128)(2,1)} fusion(bf16[1024,128]{1,0:T(8,128)(2,1)} %bitcast.60, bf16[1024,128]{1,0:T(8,128)(2,1)} %bitcast.61), kind=kLoop, calls=%fused_computation.4 | loop fusion | flops 1048576 | bytes 1048576 | tf_op jit(solution)/shard_map/concatenate | solution.py:134
  10.2 7.3 %collective-permute-start = (bf16[2,4,8192]{2,1,0:T(4,128)(2,1)S(1)}, bf16[2,4,8192]{2,1,0:T(4,128)(2,1)S(1)}, u32[]{:S(2)}, u32[]{:S(2)}) collective-permute-start(bf16[2,4,8192]{2,1,0:T(4,128)(2,1)S(1)} %pad_maximum_fusion.3), channel_id=1, source_target_pairs={{0,4},{1,5},{2,6},{3,7},{4,0},{5,1},{6,2},{7,3},{8,12},{9,13},{10,... | collective-permute-start | bytes 393224 | tf_op jit(solution)/shard_map/ppermute | solution.py:29
  17.4 3.6 %collective-permute-done = bf16[2,4,8192]{2,1,0:T(4,128)(2,1)S(1)} collective-permute-done((bf16[2,4,8192]{2,1,0:T(4,128)(2,1)S(1)}, bf16[2,4,8192]{2,1,0:T(4,128)(2,1)S(1)}, u32[]{:S(2)}, u32[]{:S(2)}) %collective-permute-start) | collective-permute-done | bytes 131104 | tf_op jit(solution)/shard_map/ppermute | solution.py:29
  22.0 2.2 %collective-permute-start.2 = (bf16[8,8192]{1,0:T(8,128)(2,1)S(1)}, bf16[8,8192]{1,0:T(8,128)(2,1)S(1)}, u32[]{:S(2)}, u32[]{:S(2)}) collective-permute-start(bf16[8,8192]{1,0:T(8,128)(2,1)S(1)} %get-tuple-element.37), channel_id=1, source_target_pairs={{0,2},{1,3},{2,0},{3,1},{4,6},{5,7},{6,4},{7,5},{8,10},{9,11},{10,... | collective-permute-start | bytes 393224 | tf_op jit(solution)/shard_map/ppermute | solution.py:29
  24.2 1.4 collective-permute-start.1
  27.1 3.3 %collective-permute-start.8 = (bf16[8,8192]{1,0:T(8,128)(2,1)S(1)}, bf16[8,8192]{1,0:T(8,128)(2,1)S(1)}, u32[]{:S(2)}, u32[]{:S(2)}) collective-permute-start(bf16[8,8192]{1,0:T(8,128)(2,1)S(1)} %get-tuple-element.33), channel_id=1, source_target_pairs={{0,16},{1,17},{2,18},{3,19},{4,20},{5,21},{6,22},{7,23},{8,24},{9,... | collective-permute-start | bytes 393224 | tf_op jit(solution)/shard_map/ppermute | solution.py:29
  30.4 1.1 collective-permute-start.7
  33.3 3.1 %collective-permute-start.5 = (bf16[4,8,8192]{2,1,0:T(8,128)(2,1)S(1)}, bf16[4,8,8192]{2,1,0:T(8,128)(2,1)S(1)}, u32[]{:S(2)}, u32[]{:S(2)}) collective-permute-start(bf16[4,8,8192]{2,1,0:T(8,128)(2,1)S(1)} %pad_maximum_fusion.refs_2_), channel_id=1, source_target_pairs={{0,16},{1,17},{2,18},{3,19},{4,20},{5,21},{6,22},{7,23},{8,24},{9,... | collective-permute-start | bytes 1572872 | tf_op jit(solution)/shard_map/ppermute | solution.py:29
  37.1 2.1 %collective-permute-done.9 = bf16[8,8192]{1,0:T(8,128)(2,1)S(1)} collective-permute-done((bf16[8,8192]{1,0:T(8,128)(2,1)S(1)}, bf16[8,8192]{1,0:T(8,128)(2,1)S(1)}, u32[]{:S(2)}, u32[]{:S(2)}) %collective-permute-start.9) | collective-permute-done | bytes 131104 | tf_op jit(solution)/shard_map/ppermute | solution.py:29
  39.3 3.5 %collective-permute-start.11 = (bf16[4,8,8192]{2,1,0:T(8,128)(2,1)S(1)}, bf16[4,8,8192]{2,1,0:T(8,128)(2,1)S(1)}, u32[]{:S(2)}, u32[]{:S(2)}) collective-permute-start(bf16[4,8,8192]{2,1,0:T(8,128)(2,1)S(1)} %pad_maximum_fusion.1.refs_6_), channel_id=1, source_target_pairs={{0,2},{1,3},{2,0},{3,1},{4,6},{5,7},{6,4},{7,5},{8,10},{9,11},{10,... | collective-permute-start | bytes 1572872 | tf_op jit(solution)/shard_map/ppermute | solution.py:29
  42.8 6.6 %collective-permute-done.6.refs_5_ = bf16[4,8,8192]{2,1,0:T(8,128)(2,1)S(1)} collective-permute-done((bf16[4,8,8192]{2,1,0:T(8,128)(2,1)S(1)}, bf16[4,8,8192]{2,1,0:T(8,128)(2,1)S(1)}, u32[]{:S(2)}, u32[]{:S(2)}) %collective-permute-start.6) | collective-permute-done | bytes 524320 | tf_op jit(solution)/shard_map/ppermute | solution.py:29
  49.4 11.4 %collective-permute-start.10 = (bf16[4,8,8192]{2,1,0:T(8,128)(2,1)S(1)}, bf16[4,8,8192]{2,1,0:T(8,128)(2,1)}, u32[]{:S(2)}, u32[]{:S(2)}) collective-permute-start(bf16[4,8,8192]{2,1,0:T(8,128)(2,1)S(1)} %pad_maximum_fusion.1.refs_6_), channel_id=1, source_target_pairs={{0,3},{1,0},{2,1},{3,2},{4,7},{5,4},{6,5},{7,6},{8,11},{9,8},{10,9... | collective-permute-start | bytes 1572872 | tf_op jit(solution)/shard_map/ppermute | solution.py:29
  62.5 5.0 %collective-permute-done.10.refs_7_ = bf16[4,8,8192]{2,1,0:T(8,128)(2,1)} collective-permute-done((bf16[4,8,8192]{2,1,0:T(8,128)(2,1)S(1)}, bf16[4,8,8192]{2,1,0:T(8,128)(2,1)}, u32[]{:S(2)}, u32[]{:S(2)}) %collective-permute-start.10) | collective-permute-done | bytes 524320 | tf_op jit(solution)/shard_map/ppermute | solution.py:29
  67.5 12.9 %shard_map.93 = (bf16[4,8,8192]{2,1,0:T(8,128)(2,1)S(1)}, bf16[4,8,8192]{2,1,0:T(8,128)(2,1)S(1)}, bf16[4,8,8192]{2,1,0:T(8,128)(2,1)S(1)}, bf16[4,8,8192]{2,1,0...) custom-call(s32[4,16]{1,0:T(4,128)S(1)} %copy-done, ...), custom_call_target="tpu_custom_call" | custom-call | flops 1700000000 | bytes 17000000 | tf_op jit(solution)/shard_map/pallas_call | solution.py:103
  80.5 1.7 %collective-permute-start.13 = (bf16[4,8,8192]{2,1,0:T(8,128)(2,1)S(1)}, bf16[4,8,8192]{2,1,0:T(8,128)(2,1)S(1)}, u32[]{:S(2)}, u32[]{:S(2)}) collective-permute-start(bf16[4,8,8192]{2,1,0:T(8,128)(2,1)S(1)} %get-tuple-element.14), channel_id=1, source_target_pairs={{0,8},{1,9},{2,10},{3,11},{4,12},{5,13},{6,14},{7,15},{8,16},{9,17... | collective-permute-start | bytes 1572872 | tf_op jit(solution)/shard_map/ppermute | solution.py:29
  82.2 2.8 %collective-permute-start.14 = (bf16[4,8,8192]{2,1,0:T(8,128)(2,1)S(1)}, bf16[4,8,8192]{2,1,0:T(8,128)(2,1)S(1)}, u32[]{:S(2)}, u32[]{:S(2)}) collective-permute-start(bf16[4,8,8192]{2,1,0:T(8,128)(2,1)S(1)} %get-tuple-element.15), channel_id=1, source_target_pairs={{0,16},{1,17},{2,18},{3,19},{4,20},{5,21},{6,22},{7,23},{8,24},{9,... | collective-permute-start | bytes 1572872 | tf_op jit(solution)/shard_map/ppermute | solution.py:29
  85.0 1.5 collective-permute-start.15
  86.5 1.5 collective-permute-start.19
  87.9 1.2 collective-permute-start.20
  89.2 6.7 %collective-permute-done.13 = bf16[4,8,8192]{2,1,0:T(8,128)(2,1)S(1)} collective-permute-done((bf16[4,8,8192]{2,1,0:T(8,128)(2,1)S(1)}, bf16[4,8,8192]{2,1,0:T(8,128)(2,1)S(1)}, u32[]{:S(2)}, u32[]{:S(2)}) %collective-permute-start.13) | collective-permute-done | bytes 524320 | tf_op jit(solution)/shard_map/ppermute | solution.py:29
  96.5 9.0 %collective-permute-done.14 = bf16[4,8,8192]{2,1,0:T(8,128)(2,1)S(1)} collective-permute-done((bf16[4,8,8192]{2,1,0:T(8,128)(2,1)S(1)}, bf16[4,8,8192]{2,1,0:T(8,128)(2,1)S(1)}, u32[]{:S(2)}, u32[]{:S(2)}) %collective-permute-start.14) | collective-permute-done | bytes 524320 | tf_op jit(solution)/shard_map/ppermute | solution.py:29
  105.5 1.3 add_convert_fusion.1
  106.8 1.5 collective-permute-start.16
  108.9 2.0 %collective-permute-start.17 = (bf16[8,8192]{1,0:T(8,128)(2,1)S(1)}, bf16[8,8192]{1,0:T(8,128)(2,1)S(1)}, u32[]{:S(2)}, u32[]{:S(2)}) collective-permute-start(bf16[8,8192]{1,0:T(8,128)(2,1)S(1)} %get-tuple-element.26), channel_id=1, source_target_pairs={{0,2},{1,3},{2,0},{3,1},{4,6},{5,7},{6,4},{7,5},{8,10},{9,11},{10,... | collective-permute-start | bytes 393224 | tf_op jit(solution)/shard_map/ppermute | solution.py:29
  111.0 1.9 %collective-permute-done.21 = bf16[4,8,8192]{2,1,0:T(8,128)(2,1)S(1)} collective-permute-done((bf16[4,8,8192]{2,1,0:T(8,128)(2,1)}, bf16[4,8,8192]{2,1,0:T(8,128)(2,1)S(1)}, u32[]{:S(2)}, u32[]{:S(2)}) %collective-permute-start.21) | collective-permute-done | bytes 524320 | tf_op jit(solution)/shard_map/ppermute | solution.py:29
  113.3 3.2 %collective-permute-start.24 = (bf16[8,8192]{1,0:T(8,128)(2,1)S(1)}, bf16[8,8192]{1,0:T(8,128)(2,1)S(1)}, u32[]{:S(2)}, u32[]{:S(2)}) collective-permute-start(bf16[8,8192]{1,0:T(8,128)(2,1)S(1)} %get-tuple-element.28), channel_id=1, source_target_pairs={{0,24},{1,25},{2,26},{3,27},{4,28},{5,29},{6,30},{7,31},{8,0},{9,1... | collective-permute-start | bytes 393224 | tf_op jit(solution)/shard_map/ppermute | solution.py:29
  116.8 2.7 %collective-permute-done.22 = bf16[8,8192]{1,0:T(8,128)(2,1)S(1)} collective-permute-done((bf16[8,8192]{1,0:T(8,128)(2,1)S(1)}, bf16[8,8192]{1,0:T(8,128)(2,1)S(1)}, u32[]{:S(2)}, u32[]{:S(2)}) %collective-permute-start.22) | collective-permute-done | bytes 131104 | tf_op jit(solution)/shard_map/ppermute | solution.py:29
  120.4 2.6 %collective-permute-done.23 = bf16[8,8192]{1,0:T(8,128)(2,1)S(1)} collective-permute-done((bf16[8,8192]{1,0:T(8,128)(2,1)S(1)}, bf16[8,8192]{1,0:T(8,128)(2,1)S(1)}, u32[]{:S(2)}, u32[]{:S(2)}) %collective-permute-start.23) | collective-permute-done | bytes 131104 | tf_op jit(solution)/shard_map/ppermute | solution.py:29
  123.2 4.7 %collective-permute-start.25 = (bf16[2,4,8192]{2,1,0:T(4,128)(2,1)S(1)}, bf16[2,4,8192]{2,1,0:T(4,128)(2,1)S(1)}, u32[]{:S(2)}, u32[]{:S(2)}) collective-permute-start(bf16[2,4,8192]{2,1,0:T(4,128)(2,1)S(1)} %pad_maximum_fusion.6), channel_id=1, source_target_pairs={{0,4},{1,5},{2,6},{3,7},{4,0},{5,1},{6,2},{7,3},{8,12},{9,13},{10,... | collective-permute-start | bytes 393224 | tf_op jit(solution)/shard_map/ppermute | solution.py:29
  127.9 8.2 %collective-permute-done.25 = bf16[2,4,8192]{2,1,0:T(4,128)(2,1)S(1)} collective-permute-done((bf16[2,4,8192]{2,1,0:T(4,128)(2,1)S(1)}, bf16[2,4,8192]{2,1,0:T(4,128)(2,1)S(1)}, u32[]{:S(2)}, u32[]{:S(2)}) %collective-permute-start.25) | collective-permute-done | bytes 131104 | tf_op jit(solution)/shard_map/ppermute | solution.py:29
  136.8 13.7 %reduce-scatter.2.cloned.1.call-done = bf16[2048,128]{1,0:T(8,128)(2,1)} async-done(((bf16[16384,128]{1,0:T(8,128)(2,1)}), bf16[2048,128]{1,0:T(8,128)(2,1)}) %reduce-scatter.2.cloned.1.call-update) | async-done | bytes 524304 | tf_op jit(solution)/shard_map/reduce_scatter | solution.py:149
  150.5 1.9 %fusion.10 = (bf16[1024,128]{1,0:T(8,128)(2,1)}, bf16[1024,128]{1,0:T(8,128)(2,1)}) fusion(bf16[2048,128]{1,0:T(8,128)(2,1)} %reduce-scatter.2.cloned.1.call-done), kind=kLoop, calls=%fused_computation.37 | loop fusion | bytes 1048576 | tf_op jit(solution)/shard_map/slice | solution.py:159
  (65 shorter events, 11.6 us)
Async XLA Ops:
  7.2 60.4 %copy-start.1 = (s32[4]{0:T(128)S(1)}, s32[4]{0:T(128)}, u32[]{:S(2)}) copy-start(s32[4]{0:T(128)} %refs_1_.1) | copy-start | bytes 52
  7.2 60.4 %copy-start = (s32[4,16]{1,0:T(4,128)S(1)}, s32[4,16]{1,0:T(4,128)}, u32[]{:S(2)}) copy-start(s32[4,16]{1,0:T(4,128)} %refs_0_.1) | copy-start | bytes 772
  7.2 60.3 %all-gather.2.cloned.1.call-start = ((), (), s32[]{:S(2)}) async-start(), calls=%async_computation.1 | async-start | bytes 4718592 | tf_op jit(solution)/shard_map/all_gather | solution.py:135
  9.1 141.4 %reduce-scatter.2.cloned.1.call-start = ((), (), s32[]{:S(2)}) async-start(), calls=%async_computation.2 | async-start | bytes 4718592 | tf_op jit(solution)/shard_map/reduce_scatter | solution.py:149
  10.2 10.9 %collective-permute-start = (bf16[2,4,8192]{2,1,0:T(4,128)(2,1)S(1)}, bf16[2,4,8192]{2,1,0:T(4,128)(2,1)S(1)}, u32[]{:S(2)}, u32[]{:S(2)}) collective-permute-start(bf16[2,4,8192]{2,1,0:T(4,128)(2,1)S(1)} %pad_maximum_fusion.3), channel_id=1, source_target_pairs={{0,4},{1,5},{2,6},{3,7},{4,0},{5,1},{6,2},{7,3},{8,12},{9,13},{10,... | collective-permute-start | bytes 393224 | tf_op jit(solution)/shard_map/ppermute | solution.py:29
  22.0 9.5 %collective-permute-start.2 = (bf16[8,8192]{1,0:T(8,128)(2,1)S(1)}, bf16[8,8192]{1,0:T(8,128)(2,1)S(1)}, u32[]{:S(2)}, u32[]{:S(2)}) collective-permute-start(bf16[8,8192]{1,0:T(8,128)(2,1)S(1)} %get-tuple-element.37), channel_id=1, source_target_pairs={{0,2},{1,3},{2,0},{3,1},{4,6},{5,7},{6,4},{7,5},{8,10},{9,11},{10,... | collective-permute-start | bytes 393224 | tf_op jit(solution)/shard_map/ppermute | solution.py:29
  24.2 8.3 %collective-permute-start.1 = (bf16[8,8192]{1,0:T(8,128)(2,1)S(1)}, bf16[8,8192]{1,0:T(8,128)(2,1)S(1)}, u32[]{:S(2)}, u32[]{:S(2)}) collective-permute-start(bf16[8,8192]{1,0:T(8,128)(2,1)S(1)} %get-tuple-element.37), channel_id=1, source_target_pairs={{0,3},{1,0},{2,1},{3,2},{4,7},{5,4},{6,5},{7,6},{8,11},{9,8},{10,9... | collective-permute-start | bytes 393224 | tf_op jit(solution)/shard_map/ppermute | solution.py:29
  25.6 6.8 %collective-permute-start.3 = (bf16[8,8192]{1,0:T(8,128)(2,1)S(1)}, bf16[8,8192]{1,0:T(8,128)(2,1)S(1)}, u32[]{:S(2)}, u32[]{:S(2)}) collective-permute-start(bf16[8,8192]{1,0:T(8,128)(2,1)S(1)} %get-tuple-element.37), channel_id=1, source_target_pairs={{0,1},{1,2},{2,3},{3,0},{4,5},{5,6},{6,7},{7,4},{8,9},{9,10},{10,1... | collective-permute-start | bytes 393224 | tf_op jit(solution)/shard_map/ppermute | solution.py:29
  27.1 9.2 %collective-permute-start.8 = (bf16[8,8192]{1,0:T(8,128)(2,1)S(1)}, bf16[8,8192]{1,0:T(8,128)(2,1)S(1)}, u32[]{:S(2)}, u32[]{:S(2)}) collective-permute-start(bf16[8,8192]{1,0:T(8,128)(2,1)S(1)} %get-tuple-element.33), channel_id=1, source_target_pairs={{0,16},{1,17},{2,18},{3,19},{4,20},{5,21},{6,22},{7,23},{8,24},{9,... | collective-permute-start | bytes 393224 | tf_op jit(solution)/shard_map/ppermute | solution.py:29
  30.4 6.6 %collective-permute-start.7 = (bf16[8,8192]{1,0:T(8,128)(2,1)S(1)}, bf16[8,8192]{1,0:T(8,128)(2,1)S(1)}, u32[]{:S(2)}, u32[]{:S(2)}) collective-permute-start(bf16[8,8192]{1,0:T(8,128)(2,1)S(1)} %get-tuple-element.33), channel_id=1, source_target_pairs={{0,24},{1,25},{2,26},{3,27},{4,28},{5,29},{6,30},{7,31},{8,0},{9,1... | collective-permute-start | bytes 393224 | tf_op jit(solution)/shard_map/ppermute | solution.py:29
  31.5 7.6 %collective-permute-start.9 = (bf16[8,8192]{1,0:T(8,128)(2,1)S(1)}, bf16[8,8192]{1,0:T(8,128)(2,1)S(1)}, u32[]{:S(2)}, u32[]{:S(2)}) collective-permute-start(bf16[8,8192]{1,0:T(8,128)(2,1)S(1)} %get-tuple-element.33), channel_id=1, source_target_pairs={{0,8},{1,9},{2,10},{3,11},{4,12},{5,13},{6,14},{7,15},{8,16},{9,17... | collective-permute-start | bytes 393224 | tf_op jit(solution)/shard_map/ppermute | solution.py:29
  32.5 35.0 %copy-start.2 = (bf16[4,8,8192]{2,1,0:T(8,128)(2,1)}, bf16[4,8,8192]{2,1,0:T(8,128)(2,1)S(1)}, u32[]{:S(2)}) copy-start(bf16[4,8,8192]{2,1,0:T(8,128)(2,1)S(1)} %pad_maximum_fusion.refs_2_) | copy-start | bytes 1572868
  32.5 16.8 %collective-permute-start.6 = (bf16[4,8,8192]{2,1,0:T(8,128)(2,1)S(1)}, bf16[4,8,8192]{2,1,0:T(8,128)(2,1)S(1)}, u32[]{:S(2)}, u32[]{:S(2)}) collective-permute-start(bf16[4,8,8192]{2,1,0:T(8,128)(2,1)S(1)} %pad_maximum_fusion.refs_2_), channel_id=1, source_target_pairs={{0,8},{1,9},{2,10},{3,11},{4,12},{5,13},{6,14},{7,15},{8,16},{9,17... | collective-permute-start | bytes 1572872 | tf_op jit(solution)/shard_map/ppermute | solution.py:29
  33.3 27.5 %collective-permute-start.5 = (bf16[4,8,8192]{2,1,0:T(8,128)(2,1)S(1)}, bf16[4,8,8192]{2,1,0:T(8,128)(2,1)S(1)}, u32[]{:S(2)}, u32[]{:S(2)}) collective-permute-start(bf16[4,8,8192]{2,1,0:T(8,128)(2,1)S(1)} %pad_maximum_fusion.refs_2_), channel_id=1, source_target_pairs={{0,16},{1,17},{2,18},{3,19},{4,20},{5,21},{6,22},{7,23},{8,24},{9,... | collective-permute-start | bytes 1572872 | tf_op jit(solution)/shard_map/ppermute | solution.py:29
  36.4 24.4 %collective-permute-start.4 = (bf16[4,8,8192]{2,1,0:T(8,128)(2,1)S(1)}, bf16[4,8,8192]{2,1,0:T(8,128)(2,1)S(1)}, u32[]{:S(2)}, u32[]{:S(2)}) collective-permute-start(bf16[4,8,8192]{2,1,0:T(8,128)(2,1)S(1)} %pad_maximum_fusion.refs_2_), channel_id=1, source_target_pairs={{0,24},{1,25},{2,26},{3,27},{4,28},{5,29},{6,30},{7,31},{8,0},{9,1... | collective-permute-start | bytes 1572872 | tf_op jit(solution)/shard_map/ppermute | solution.py:29
  39.2 21.6 %collective-permute-start.12 = (bf16[4,8,8192]{2,1,0:T(8,128)(2,1)S(1)}, bf16[4,8,8192]{2,1,0:T(8,128)(2,1)S(1)}, u32[]{:S(2)}, u32[]{:S(2)}) collective-permute-start(bf16[4,8,8192]{2,1,0:T(8,128)(2,1)S(1)} %pad_maximum_fusion.1.refs_6_), channel_id=1, source_target_pairs={{0,1},{1,2},{2,3},{3,0},{4,5},{5,6},{6,7},{7,4},{8,9},{9,10},{10,1... | collective-permute-start | bytes 1572872 | tf_op jit(solution)/shard_map/ppermute | solution.py:29
  39.3 21.5 %collective-permute-start.11 = (bf16[4,8,8192]{2,1,0:T(8,128)(2,1)S(1)}, bf16[4,8,8192]{2,1,0:T(8,128)(2,1)S(1)}, u32[]{:S(2)}, u32[]{:S(2)}) collective-permute-start(bf16[4,8,8192]{2,1,0:T(8,128)(2,1)S(1)} %pad_maximum_fusion.1.refs_6_), channel_id=1, source_target_pairs={{0,2},{1,3},{2,0},{3,1},{4,6},{5,7},{6,4},{7,5},{8,10},{9,11},{10,... | collective-permute-start | bytes 1572872 | tf_op jit(solution)/shard_map/ppermute | solution.py:29
  49.4 18.1 %collective-permute-start.10 = (bf16[4,8,8192]{2,1,0:T(8,128)(2,1)S(1)}, bf16[4,8,8192]{2,1,0:T(8,128)(2,1)}, u32[]{:S(2)}, u32[]{:S(2)}) collective-permute-start(bf16[4,8,8192]{2,1,0:T(8,128)(2,1)S(1)} %pad_maximum_fusion.1.refs_6_), channel_id=1, source_target_pairs={{0,3},{1,0},{2,1},{3,2},{4,7},{5,4},{6,5},{7,6},{8,11},{9,8},{10,9... | collective-permute-start | bytes 1572872 | tf_op jit(solution)/shard_map/ppermute | solution.py:29
  80.5 32.4 %copy-start.4 = (bf16[4,8,8192]{2,1,0:T(8,128)(2,1)S(1)}, bf16[4,8,8192]{2,1,0:T(8,128)(2,1)}, u32[]{:S(2)}) copy-start(bf16[4,8,8192]{2,1,0:T(8,128)(2,1)} %get-tuple-element.17) | copy-start | bytes 1572868
  80.5 15.4 %collective-permute-start.13 = (bf16[4,8,8192]{2,1,0:T(8,128)(2,1)S(1)}, bf16[4,8,8192]{2,1,0:T(8,128)(2,1)S(1)}, u32[]{:S(2)}, u32[]{:S(2)}) collective-permute-start(bf16[4,8,8192]{2,1,0:T(8,128)(2,1)S(1)} %get-tuple-element.14), channel_id=1, source_target_pairs={{0,8},{1,9},{2,10},{3,11},{4,12},{5,13},{6,14},{7,15},{8,16},{9,17... | collective-permute-start | bytes 1572872 | tf_op jit(solution)/shard_map/ppermute | solution.py:29
  82.2 23.2 %collective-permute-start.14 = (bf16[4,8,8192]{2,1,0:T(8,128)(2,1)S(1)}, bf16[4,8,8192]{2,1,0:T(8,128)(2,1)S(1)}, u32[]{:S(2)}, u32[]{:S(2)}) collective-permute-start(bf16[4,8,8192]{2,1,0:T(8,128)(2,1)S(1)} %get-tuple-element.15), channel_id=1, source_target_pairs={{0,16},{1,17},{2,18},{3,19},{4,20},{5,21},{6,22},{7,23},{8,24},{9,... | collective-permute-start | bytes 1572872 | tf_op jit(solution)/shard_map/ppermute | solution.py:29
  85.0 20.5 %collective-permute-start.15 = (bf16[4,8,8192]{2,1,0:T(8,128)(2,1)}, bf16[4,8,8192]{2,1,0:T(8,128)(2,1)}, u32[]{:S(2)}, u32[]{:S(2)}) collective-permute-start(bf16[4,8,8192]{2,1,0:T(8,128)(2,1)} %get-tuple-element.16), channel_id=1, source_target_pairs={{0,24},{1,25},{2,26},{3,27},{4,28},{5,29},{6,30},{7,31},{8,0},{9,1... | collective-permute-start | bytes 1572872 | tf_op jit(solution)/shard_map/ppermute | solution.py:29
  86.5 22.5 %collective-permute-start.19 = (bf16[4,8,8192]{2,1,0:T(8,128)(2,1)}, bf16[4,8,8192]{2,1,0:T(8,128)(2,1)S(1)}, u32[]{:S(2)}, u32[]{:S(2)}) collective-permute-start(bf16[4,8,8192]{2,1,0:T(8,128)(2,1)} %get-tuple-element.18), channel_id=1, source_target_pairs={{0,1},{1,2},{2,3},{3,0},{4,5},{5,6},{6,7},{7,4},{8,9},{9,10},{10,1... | collective-permute-start | bytes 1572872 | tf_op jit(solution)/shard_map/ppermute | solution.py:29
  87.9 23.0 %collective-permute-start.20 = (bf16[4,8,8192]{2,1,0:T(8,128)(2,1)}, bf16[4,8,8192]{2,1,0:T(8,128)(2,1)S(1)}, u32[]{:S(2)}, u32[]{:S(2)}) collective-permute-start(bf16[4,8,8192]{2,1,0:T(8,128)(2,1)} %get-tuple-element.19), channel_id=1, source_target_pairs={{0,2},{1,3},{2,0},{3,1},{4,6},{5,7},{6,4},{7,5},{8,10},{9,11},{10,... | collective-permute-start | bytes 1572872 | tf_op jit(solution)/shard_map/ppermute | solution.py:29
  95.9 17.0 %collective-permute-start.21 = (bf16[4,8,8192]{2,1,0:T(8,128)(2,1)}, bf16[4,8,8192]{2,1,0:T(8,128)(2,1)S(1)}, u32[]{:S(2)}, u32[]{:S(2)}) collective-permute-start(bf16[4,8,8192]{2,1,0:T(8,128)(2,1)} %get-tuple-element.20), channel_id=1, source_target_pairs={{0,3},{1,0},{2,1},{3,2},{4,7},{5,4},{6,5},{7,6},{8,11},{9,8},{10,9... | collective-permute-start | bytes 1572872 | tf_op jit(solution)/shard_map/ppermute | solution.py:29
  106.8 9.7 %collective-permute-start.16 = (bf16[8,8192]{1,0:T(8,128)(2,1)S(1)}, bf16[8,8192]{1,0:T(8,128)(2,1)S(1)}, u32[]{:S(2)}, u32[]{:S(2)}) collective-permute-start(bf16[8,8192]{1,0:T(8,128)(2,1)S(1)} %get-tuple-element.24), channel_id=1, source_target_pairs={{0,1},{1,2},{2,3},{3,0},{4,5},{5,6},{6,7},{7,4},{8,9},{9,10},{10,1... | collective-permute-start | bytes 393224 | tf_op jit(solution)/shard_map/ppermute | solution.py:29
  108.3 8.2 %collective-permute-start.18 = (bf16[8,8192]{1,0:T(8,128)(2,1)S(1)}, bf16[8,8192]{1,0:T(8,128)(2,1)S(1)}, u32[]{:S(2)}, u32[]{:S(2)}) collective-permute-start(bf16[8,8192]{1,0:T(8,128)(2,1)S(1)} %get-tuple-element.25), channel_id=1, source_target_pairs={{0,3},{1,0},{2,1},{3,2},{4,7},{5,4},{6,5},{7,6},{8,11},{9,8},{10,9... | collective-permute-start | bytes 393224 | tf_op jit(solution)/shard_map/ppermute | solution.py:29
  108.9 7.8 %collective-permute-start.17 = (bf16[8,8192]{1,0:T(8,128)(2,1)S(1)}, bf16[8,8192]{1,0:T(8,128)(2,1)S(1)}, u32[]{:S(2)}, u32[]{:S(2)}) collective-permute-start(bf16[8,8192]{1,0:T(8,128)(2,1)S(1)} %get-tuple-element.26), channel_id=1, source_target_pairs={{0,2},{1,3},{2,0},{3,1},{4,6},{5,7},{6,4},{7,5},{8,10},{9,11},{10,... | collective-permute-start | bytes 393224 | tf_op jit(solution)/shard_map/ppermute | solution.py:29
  113.2 6.4 %collective-permute-start.22 = (bf16[8,8192]{1,0:T(8,128)(2,1)S(1)}, bf16[8,8192]{1,0:T(8,128)(2,1)S(1)}, u32[]{:S(2)}, u32[]{:S(2)}) collective-permute-start(bf16[8,8192]{1,0:T(8,128)(2,1)S(1)} %get-tuple-element.27), channel_id=1, source_target_pairs={{0,8},{1,9},{2,10},{3,11},{4,12},{5,13},{6,14},{7,15},{8,16},{9,17... | collective-permute-start | bytes 393224 | tf_op jit(solution)/shard_map/ppermute | solution.py:29
  113.3 7.1 %collective-permute-start.24 = (bf16[8,8192]{1,0:T(8,128)(2,1)S(1)}, bf16[8,8192]{1,0:T(8,128)(2,1)S(1)}, u32[]{:S(2)}, u32[]{:S(2)}) collective-permute-start(bf16[8,8192]{1,0:T(8,128)(2,1)S(1)} %get-tuple-element.28), channel_id=1, source_target_pairs={{0,24},{1,25},{2,26},{3,27},{4,28},{5,29},{6,30},{7,31},{8,0},{9,1... | collective-permute-start | bytes 393224 | tf_op jit(solution)/shard_map/ppermute | solution.py:29
  116.5 6.5 %collective-permute-start.23 = (bf16[8,8192]{1,0:T(8,128)(2,1)S(1)}, bf16[8,8192]{1,0:T(8,128)(2,1)S(1)}, u32[]{:S(2)}, u32[]{:S(2)}) collective-permute-start(bf16[8,8192]{1,0:T(8,128)(2,1)S(1)} %get-tuple-element.29), channel_id=1, source_target_pairs={{0,16},{1,17},{2,18},{3,19},{4,20},{5,21},{6,22},{7,23},{8,24},{9,... | collective-permute-start | bytes 393224 | tf_op jit(solution)/shard_map/ppermute | solution.py:29
  123.2 12.9 %collective-permute-start.25 = (bf16[2,4,8192]{2,1,0:T(4,128)(2,1)S(1)}, bf16[2,4,8192]{2,1,0:T(4,128)(2,1)S(1)}, u32[]{:S(2)}, u32[]{:S(2)}) collective-permute-start(bf16[2,4,8192]{2,1,0:T(4,128)(2,1)S(1)} %pad_maximum_fusion.6), channel_id=1, source_target_pairs={{0,4},{1,5},{2,6},{3,7},{4,0},{5,1},{6,2},{7,3},{8,12},{9,13},{10,... | collective-permute-start | bytes 393224 | tf_op jit(solution)/shard_map/ppermute | solution.py:29
  (6 other events, 61.5 us)
Sparse Core Ops, SparseCore 0:
  9.8 57.6 all-gather.1
  86.6 63.8 reduce-scatter.1
